TPU v7x, 512 devices: a whole 4x4x16 slice. The times are simulated.
512 devices in a mesh: ev: 64 (over z, y), st: 8 (over x, core).
Axes of the slice: x: 4, y: 4, z: 16, core: 2. Of those that a mesh axis runs over, the one named last changes fastest.
Arguments:
- records: bfloat16 [256, 144, 3, 1024], P('ev', 'st'), may hold values from -6 to 6
- store: bfloat16 [64, 6, 144, 3, 1024], P('ev', None, 'st'), may hold values from -0.0014648438 to 0.0014648438
- taper: float32 [256], replicated, may hold values from 0.1 to 1
- candidates: int32 [256, 16], P('ev'), may hold values from 0 to 63, as said below
- node_slot: int32 [64], replicated, may hold values from 0 to 63, as said below
Outputs:
- moment: float32 [256, 16, 6], P('ev')
Inputs may be any that keep to these rules, and one draw needn't show every extreme that they name: Node ids. Of the 64 candidates of the events of one index of ev (aligned blocks of 4 events), at most 2 map to the same store row (node_slot[id]), and in every block some store row is taken by exactly 2. An event may list a node more than once. `node_slot`: A permutation of 0 to 63.
All inputs are finite; a program needn't handle non-finite values.
Results may differ from a plain program's by a relative error of at most 0.005.
Values may be sent and summed in bfloat16 or wider, within the bound.
A program may use at most 64 MiB of HBM per device.

v0:
```python
import math

import jax
import jax.numpy as jnp
from jax import lax
from jax.sharding import PartitionSpec as P


def band_table(samples, freq_bins):
    sample_idx = jnp.arange(samples, dtype=jnp.int32)[:, None]
    bin_idx = jnp.arange(1, freq_bins + 1, dtype=jnp.int32)[None, :]
    phases = sample_idx * bin_idx % samples
    angles = phases.astype(jnp.float32) * (2.0 * math.pi / samples)
    return jnp.concatenate([jnp.cos(angles), -jnp.sin(angles)], axis=1).astype(jnp.bfloat16)


def spectra_of(traces, dft_table):
    samples = traces.shape[-1]
    result = jnp.dot(traces.reshape(-1, samples), dft_table, preferred_element_type=jnp.float32)
    return result.reshape(traces.shape[:-1] + (dft_table.shape[1],))


def trace_scale(traces):
    values = traces.astype(jnp.float32)
    return lax.rsqrt(jnp.mean(values * values, axis=-1, keepdims=True) + 1e-05) / math.sqrt(
        traces.shape[-1]
    )


def solve_small(matrix, target):
    extent = target.shape[-1]
    factor = {}
    for row_at in range(extent):
        for col_at in range(row_at + 1):
            running = matrix[..., row_at, col_at]
            for mid_at in range(col_at):
                running = running - factor[row_at, mid_at] * factor[col_at, mid_at]
            if row_at == col_at:
                factor[row_at, col_at] = jnp.sqrt(running)
            else:
                factor[row_at, col_at] = running / factor[col_at, col_at]
    forward = []
    for row_at in range(extent):
        running = target[..., row_at]
        for mid_at in range(row_at):
            running = running - factor[row_at, mid_at] * forward[mid_at]
        forward.append(running / factor[row_at, row_at])
    answer = [None] * extent
    for row_at in reversed(range(extent)):
        running = forward[row_at]
        for mid_at in range(row_at + 1, extent):
            running = running - factor[mid_at, row_at] * answer[mid_at]
        answer[row_at] = running / factor[row_at, row_at]
    return jnp.stack(answer, axis=-1)


def shards(records, store, taper, candidates, node_slot):
    dft_table = band_table(records.shape[-1], taper.shape[0])
    doubled = jnp.concatenate([taper, taper])
    observed = (spectra_of(records, dft_table) * trace_scale(records)).astype(jnp.bfloat16)
    ev_local = records.shape[0]
    width_flat = observed.shape[1] * observed.shape[2] * observed.shape[3]
    observed_flat = observed.reshape(ev_local, width_flat)
    node_count = store.shape[0]
    weighted = (spectra_of(store, dft_table) * doubled).astype(jnp.bfloat16)
    weighted_nodes = weighted.reshape(node_count, 6, width_flat)
    weighted_flat = weighted.reshape(node_count * 6, width_flat)
    gram_part = jnp.einsum(
        "nkf,nlf->nkl", weighted_nodes, weighted_nodes, preferred_element_type=jnp.float32
    )
    groups = lax.axis_size("ev")
    cand_count = candidates.shape[1]
    pair_count = ev_local * cand_count
    capacity = max(2, pair_count // groups + max(1, pair_count // (2 * groups)))
    slot_count = groups * capacity
    all_nodes = node_slot.shape[0]
    flat_cand = candidates.reshape(pair_count)
    matches = flat_cand[:, None] == jnp.arange(all_nodes, dtype=jnp.int32)[None, :]
    store_row = jnp.sum(jnp.where(matches, node_slot[None, :], 0), axis=1)
    owner_group = store_row // node_count
    local_row = store_row % node_count
    pair_index = jnp.arange(pair_count, dtype=jnp.int32)
    earlier = (owner_group[:, None] == owner_group[None, :]) & (
        pair_index[None, :] < pair_index[:, None]
    )
    position = jnp.sum(earlier.astype(jnp.int32), axis=1)
    slot_of_pair = owner_group * capacity + position
    slot_match = slot_of_pair[None, :] == jnp.arange(slot_count, dtype=jnp.int32)[:, None]
    event_match = (pair_index // cand_count)[:, None] == jnp.arange(ev_local, dtype=jnp.int32)[
        None, :
    ]
    selector = jnp.dot(
        slot_match.astype(jnp.bfloat16),
        event_match.astype(jnp.bfloat16),
        preferred_element_type=jnp.float32,
    ).astype(jnp.bfloat16)
    outgoing = jnp.dot(selector, observed_flat, preferred_element_type=jnp.float32).astype(
        jnp.bfloat16
    )
    outgoing = outgoing.reshape(groups, capacity, width_flat)
    slot_nodes = jnp.max(jnp.where(slot_match, local_row[None, :], -1), axis=1).reshape(
        groups, capacity
    )
    spectra_in = lax.all_to_all(outgoing, "ev", split_axis=0, concat_axis=0, tiled=True)
    nodes_in = lax.all_to_all(slot_nodes, "ev", split_axis=0, concat_axis=0, tiled=True)
    leading = spectra_in.shape[0]
    items = spectra_in.shape[1]
    products = jnp.dot(
        spectra_in.reshape(leading * items, width_flat),
        weighted_flat.T,
        preferred_element_type=jnp.float32,
    )
    products = products.reshape(leading, items, node_count, 6)
    picked = nodes_in[..., None] == jnp.arange(node_count, dtype=jnp.int32)
    partial_value = jnp.sum(jnp.where(picked[..., None], products, 0.0), axis=2)
    node_pick = nodes_in[..., None] == jnp.arange(node_count, dtype=jnp.int32)
    proj_sum, gram_sum = lax.psum((partial_value, gram_part), "st")
    gram_slot = jnp.sum(jnp.where(node_pick[..., None, None], gram_sum[None, None], 0.0), axis=2)
    valid = nodes_in >= 0
    gram_slot = jnp.where(valid[..., None, None], gram_slot, jnp.eye(6, dtype=jnp.float32))
    moments = solve_small(gram_slot, proj_sum)
    returned = lax.all_to_all(moments, "ev", split_axis=0, concat_axis=0, tiled=True)
    per_pair = jnp.take(returned.reshape(slot_count, 6), slot_of_pair, axis=0)
    return per_pair.reshape(ev_local, cand_count, 6)


def solution(mesh):
    return jax.shard_map(
        shards,
        mesh=mesh,
        in_specs=(
            P("ev", "st", None, None),
            P("ev", None, "st", None, None),
            P(),
            P("ev", None),
            P(),
        ),
        out_specs=P("ev", None, None),
        check_vma=False,
    )
```

profile of v0, /device:TPU:1, one launch (start us, length us, event | category | flops | bytes accessed | tf_op | source)
XLA Modules:
  0.0 423.2 jit_solution(234995035465707532)
XLA Ops:
  0.0 0.8 eq.80
  0.8 0.8 select_reduce_fusion.1
  1.6 0.2 convert_reduce_fusion
  1.9 0.8 all_to_all.12
  2.7 19.3 %all-to-all-start = ((s32[64,1,2]{2,1,0:T(1,128)}), s32[64,1,2]{2,1,0:T(1,128)S(1)}, u32[]{:S(2)}, u32[]{:S(2)}) async-start(s32[64,1,2]{2,1,0:T(1,128)} %bitcast), calls=%async_computation | async-start | bytes 65536 | tf_op jit(solution)/shard_map/all_to_all | solution.py:105
  22.0 1.3 multiply_reduce_fusion
  23.3 1.3 copy.193
  24.6 0.1 copy.194
  24.7 0.1 copy.195
  24.9 0.4 reshape.1199
  25.2 4.4 %cosine_convert_fusion = (bf16[1024,256]{1,0:T(8,128)(2,1)S(1)}, bf16[1024,256]{1,0:T(8,128)(2,1)S(1)}) fusion(s32[256]{0:T(256)S(1)} %iota_add_fusion), kind=kLoop, calls=%fused_computation.17 | loop fusion | flops 4456448 | bytes 1049600 | tf_op jit(solution)/shard_map/convert
  29.7 0.4 convolution_bitcast_fusion
  30.1 0.3 reshape.1200
  30.4 0.1 mul.1223
  30.5 4.6 %convolution_convert_fusion = bf16[128,27648]{1,0:T(8,128)(2,1)} fusion(f32[4,27648]{1,0:T(4,128)S(1)} %reshape.1200, f32[4,27648]{1,0:T(4,128)S(1)} %bitcast.279, s32[64]{0:T(128)S(1)} %and_select_fusion, s32[64]{0:T(128)S(1)} %get-tuple-element.8), kind=kOutput, calls=%fused_computation.1 | convolution fusion | flops 32146176 | bytes 7963136 | tf_op jit(solution)/shard_map/dot_general | solution.py:97
  35.1 9.2 %reshape.1201 = bf16[64,2,27648]{2,1,0:T(2,128)(2,1)} reshape(bf16[128,27648]{1,0:T(8,128)(2,1)} %convolution_convert_fusion) | data formatting | bytes 14155776 | tf_op jit(solution)/shard_map/reshape | solution.py:100
  44.3 14.9 %all-to-all-start.1 = ((bf16[64,2,27648]{2,1,0:T(2,128)(2,1)}), bf16[64,2,27648]{2,1,0:T(2,128)(2,1)}, u32[]{:S(2)}, u32[]{:S(2)}) async-start(bf16[64,2,27648]{2,1,0:T(2,128)(2,1)} %reshape.1201), calls=%async_computation.1 | async-start | bytes 14155776 | tf_op jit(solution)/shard_map/all_to_all | solution.py:104
  59.3 0.6 reshape.1202
  59.9 0.5 fusion.3
  60.4 0.4 reshape.1213
  60.8 0.4 convert_element_type.52
  61.2 0.3 fusion.80
  61.6 303.6 %all-to-all-done.1 = bf16[64,2,27648]{2,1,0:T(2,128)(2,1)} async-done(((bf16[64,2,27648]{2,1,0:T(2,128)(2,1)}), bf16[64,2,27648]{2,1,0:T(2,128)(2,1)}, u32[]{:S(2)}, u32[]{:S(2)}) %all-to-all-start.1) | async-done | bytes 7077920 | tf_op jit(solution)/shard_map/all_to_all | solution.py:104
  365.2 5.8 %fusion = f32[64,2,6]{0,2,1:T(8,128)S(1)} fusion(bf16[6,27648,1]{1,0,2:T(8,128)(2,1)S(1)} %reshape.1213, bf16[64,2,27648]{2,1,0:T(2,128)(2,1)} %all-to-all-done.1), kind=kOutput, calls=%fused_computation.2 | convolution fusion | flops 42467328 | bytes 7412736 | tf_op jit(solution)/shard_map/dot_general | solution.py:108
  371.1 28.6 %all-reduce = (f32[64,2,6]{0,1,2:T(2,128)S(1)}, f32[6,6]{1,0:T(8,128)S(1)}) all-reduce(f32[64,2,6]{0,1,2:T(2,128)S(1)} %copy_select_fusion, f32[6,6]{1,0:T(8,128)S(1)} %fusion.80), channel_id=1, replica_groups=mesh['ev'=64,'st'=8] {'st'}, use_global_device_ids=true, to_apply=%region_4.5 | all-reduce | flops 804 | bytes 6432 | tf_op jit(solution)/shard_map/psum | solution.py:117
  399.7 0.1 select_select_fusion
  400.1 0.7 copy.199
  400.8 7.1 %all-to-all-start.2 = ((f32[64,2,6]{2,1,0:T(2,128)}), f32[64,2,6]{2,1,0:T(2,128)S(1)}, u32[]{:S(2)}, u32[]{:S(2)}) async-start(f32[64,2,6]{2,1,0:T(2,128)} %copy.199), calls=%async_computation.2 | async-start | bytes 131072 | tf_op jit(solution)/shard_map/all_to_all | solution.py:122
  407.9 14.0 %all-to-all-done.2 = f32[64,2,6]{2,1,0:T(2,128)S(1)} async-done(((f32[64,2,6]{2,1,0:T(2,128)}), f32[64,2,6]{2,1,0:T(2,128)S(1)}, u32[]{:S(2)}, u32[]{:S(2)}) %all-to-all-start.2) | async-done | bytes 3104 | tf_op jit(solution)/shard_map/all_to_all | solution.py:122
  421.9 0.6 gather_fusion
  422.5 0.1 copy.200
  422.6 0.6 broadcast_select_fusion
  (26 shorter events, 0.6 us)
Async XLA Ops:
  2.7 41.6 %all-to-all-start = ((s32[64,1,2]{2,1,0:T(1,128)}), s32[64,1,2]{2,1,0:T(1,128)S(1)}, u32[]{:S(2)}, u32[]{:S(2)}) async-start(s32[64,1,2]{2,1,0:T(1,128)} %bitcast), calls=%async_computation | async-start | bytes 65536 | tf_op jit(solution)/shard_map/all_to_all | solution.py:105
  44.3 15.0 %copy-start = (bf16[1,6,18,3,1024]{4,3,2,1,0:T(4,128)(2,1)S(1)}, bf16[1,6,18,3,1024]{4,3,2,1,0:T(4,128)(2,1)}, u32[]{:S(2)}) copy-start(bf16[1,6,18,3,1024]{4,3,2,1,0:T(4,128)(2,1)} %param.6) | copy-start | bytes 1990660
  44.3 15.6 %copy-start.1 = (f32[256]{0:T(256)S(1)}, f32[256]{0:T(256)}, u32[]{:S(2)}) copy-start(f32[256]{0:T(256)} %param.7) | copy-start | bytes 3076
  44.3 320.9 %all-to-all-start.1 = ((bf16[64,2,27648]{2,1,0:T(2,128)(2,1)}), bf16[64,2,27648]{2,1,0:T(2,128)(2,1)}, u32[]{:S(2)}, u32[]{:S(2)}) async-start(bf16[64,2,27648]{2,1,0:T(2,128)(2,1)} %reshape.1201), calls=%async_computation.1 | async-start | bytes 14155776 | tf_op jit(solution)/shard_map/all_to_all | solution.py:104
  400.8 21.1 %all-to-all-start.2 = ((f32[64,2,6]{2,1,0:T(2,128)}), f32[64,2,6]{2,1,0:T(2,128)S(1)}, u32[]{:S(2)}, u32[]{:S(2)}) async-start(f32[64,2,6]{2,1,0:T(2,128)} %copy.199), calls=%async_computation.2 | async-start | bytes 131072 | tf_op jit(solution)/shard_map/all_to_all | solution.py:122
where the time goes:
time: 426 us; the launch traced here: 423 us
  waiting for transfers between devices  318 us (75%)
  starting transfers between devices  41.2 us (10%)
  blocking collectives  28.6 us (7%)
  local copies, waits for them, and re-layouts  16 us (4%)
  matrix products  11.7 us (3%)
  other arithmetic  7.88 us (2%)
    all_to_all x1, waiting for transfers between devices, shards(): lax.all_to_all(outgoing, 'ev', split_axis=0, concat_axis=0, tiled=True)  304 us
    psum x1, blocking collectives, shards(): proj_sum, gram_sum = lax.psum((partial_value, gram_part), 'st')  28.6 us
    all_to_all x1, starting transfers between devices, shards(): lax.all_to_all(slot_nodes, 'ev', split_axis=0, concat_axis=0, tiled=True)  19.3 us
    all_to_all x1, starting transfers between devices, shards(): lax.all_to_all(outgoing, 'ev', split_axis=0, concat_axis=0, tiled=True)  14.9 us
    all_to_all x1, waiting for transfers between devices, shards(): lax.all_to_all(moments, 'ev', split_axis=0, concat_axis=0, tiled=True)  14 us
    reshape x1, local copies, waits for them, and re-layouts, shards(): outgoing = outgoing.reshape(groups, capacity, width_flat)  9.19 us
  transfers between devices with their start and end apart: 3, of which 2 were waited for; matrix products, arithmetic and copies ran while one was open for 6% of the time, Pallas kernels for 0%

commit v1 on v0

v1 whole, which is shorter than its diff:
```python
import functools
import math

import jax
import jax.numpy as jnp
import numpy as np
from jax import lax
from jax.experimental import pallas as pl
from jax.experimental.pallas import tpu as pltpu
from jax.sharding import PartitionSpec as P

LANES = 128
UNITS = 8
MESH = pl.DeviceIdType.MESH


def band_table(samples, freq_bins):
    sample_idx = np.arange(samples, dtype=np.int32)[:, None]
    bin_idx = np.arange(1, freq_bins + 1, dtype=np.int32)[None, :]
    phases = sample_idx * bin_idx % samples
    angles = phases.astype(np.float32) * np.float32(2.0 * math.pi / samples)
    table = np.concatenate([np.cos(angles), -np.sin(angles)], axis=1)
    return table.astype(jnp.bfloat16)


def owner_chip(owner, core, owners, groups):
    return ((2 * owner + core) * groups) // (2 * owners)


def kernel(
    dims,
    records_hbm,
    store_hbm,
    table_hbm,
    taper_ref,
    cand_ref,
    slot_ref,
    out_ref,
    records_v,
    store_v,
    table_v,
    spectra,
    bands_a,
    bands_b,
    send_a,
    send_b,
    recv_a,
    recv_b,
    wide_a,
    wide_b,
    matrix,
    mixed,
    parts_out,
    parts_in,
    gram_slots,
    sum_slots,
    load_sem,
    gram_send,
    gram_recv,
    a_send,
    a_recv,
    b_send,
    b_recv,
    c_send,
    c_recv,
    s_send,
    s_recv,
):
    groups, members, events, elements, traces, owners, cand_count, nodes = dims
    me = lax.axis_index("ev")
    st = lax.axis_index("st")
    core = lax.rem(st, 2)
    units = traces * 4
    f32 = jnp.float32
    bf16 = jnp.bfloat16

    loads = [
        pltpu.make_async_copy(table_hbm, table_v, load_sem.at[0]),
        pltpu.make_async_copy(store_hbm, store_v, load_sem.at[1]),
        pltpu.make_async_copy(records_hbm, records_v, load_sem.at[2]),
    ]
    for load in loads:
        load.start()

    barrier = pltpu.get_barrier_semaphore()

    @pl.loop(1, members)
    def _(step):
        peer = lax.rem(st + step, members)
        pl.semaphore_signal(barrier, inc=1, device_id=(me, peer), device_id_type=MESH)

    @pl.loop(1, groups)
    def _(step):
        peer = lax.rem(me + step, groups)
        pl.semaphore_signal(barrier, inc=1, device_id=(peer, st), device_id_type=MESH)

    ranked = (2 * owners * me + groups - 1) // groups
    is_owner = (
        (ranked < 2 * owners)
        & ((ranked * groups) // (2 * owners) == me)
        & (lax.rem(ranked, 2) == core)
    )
    my_owner = ranked // 2
    first = (me * owners) // groups

    loads[0].wait()
    loads[1].wait()
    spectra[...] = jnp.dot(store_v[...], table_v[...], preferred_element_type=f32)
    for tile in range(4):
        half = (tile % 2) * LANES
        gains = taper_ref[:, half : half + LANES]
        for element in range(elements):
            block = spectra[
                element * traces : (element + 1) * traces, tile * LANES : (tile + 1) * LANES
            ]
            start = element * units + tile * traces
            bands_b[start : start + traces, :] = (block * gains).astype(bf16).astype(f32)
    pair_at = {}
    for row in range(elements):
        for col in range(row + 1):
            pair_at[row, col] = len(pair_at)
    shares = []
    for (row, col), _ in pair_at.items():
        product = (
            bands_b[row * units : (row + 1) * units, :]
            * bands_b[col * units : (col + 1) * units, :]
        )
        shares.append(jnp.sum(product, axis=0, keepdims=True))
    gram_rows = gram_slots.shape[1]
    shares.append(jnp.zeros((gram_rows - len(shares), LANES), f32))
    gram_slots[st] = jnp.concatenate(shares, axis=0)

    pl.semaphore_wait(barrier, groups + members - 2)

    def gram_copy(step):
        return pltpu.make_async_remote_copy(
            src_ref=gram_slots.at[st],
            dst_ref=gram_slots.at[st],
            send_sem=gram_send,
            recv_sem=gram_recv,
            device_id=(me, lax.rem(st + step, members)),
            device_id_type=MESH,
        )

    @pl.loop(1, members)
    def _(step):
        gram_copy(step).start()

    loads[2].wait()
    values = records_v[...].astype(f32)
    samples = values.shape[1]
    mean = jnp.sum(values * values, axis=1, keepdims=True) * (1.0 / samples)
    scale = lax.rsqrt(mean + 1e-05) * (1.0 / math.sqrt(samples))
    spectra[0 : events * traces, :] = (
        jnp.dot(records_v[...], table_v[...], preferred_element_type=f32) * scale
    )
    for tile in range(4):
        for event in range(events):
            block = spectra[
                event * traces : (event + 1) * traces, tile * LANES : (tile + 1) * LANES
            ]
            start = event * units + tile * traces
            bands_a[start : start + traces, :] = block

    def send_block(buffer, slots, owner, send_sem, recv_sem):
        chip = owner_chip(owner, core, owners, groups)

        @pl.when(chip != me)
        def _():
            pltpu.make_async_remote_copy(
                src_ref=buffer.at[owner],
                dst_ref=slots.at[me],
                send_sem=send_sem,
                recv_sem=recv_sem,
                device_id=(chip, st),
                device_id_type=MESH,
            ).start()

        @pl.when(chip == me)
        def _():
            slots[me] = buffer[owner]

    def rows_of(index, owner):
        return pl.ds(pl.multiple_of(index * units + owner * UNITS, UNITS), UNITS)

    @pl.loop(0, owners)
    def _(step):
        owner = lax.rem(first + step, owners)
        for pair in range(events // 2):
            tile = jnp.concatenate(
                [bands_a[rows_of(2 * pair, owner), :], bands_a[rows_of(2 * pair + 1, owner), :]],
                axis=0,
            )
            send_a[owner, 2 * UNITS * pair : 2 * UNITS * (pair + 1), :] = tile.astype(bf16)
        send_block(send_a, recv_a, owner, a_send, a_recv)

    others = gram_slots.at[pl.ds(0, members - 1)]
    pltpu.make_async_copy(others, others, gram_recv).wait()
    total = gram_slots[0]
    for member in range(1, members):
        total = total + gram_slots[member]
    total = jnp.broadcast_to(jnp.sum(total, axis=1, keepdims=True), total.shape)
    factor = {}
    inverse = []
    for row in range(elements):
        for col in range(row + 1):
            at = pair_at[row, col]
            running = total[at : at + 1, :]
            for mid in range(col):
                running = running - factor[row, mid] * factor[col, mid]
            if row == col:
                root = jnp.sqrt(running)
                inverse.append(1.0 / root)
            else:
                factor[row, col] = running * inverse[col]
    factor = {at: jnp.broadcast_to(value, (UNITS, LANES)) for at, value in factor.items()}
    inverse = [jnp.broadcast_to(value, (UNITS, LANES)) for value in inverse]

    @pl.loop(0, owners)
    def _(step):
        owner = lax.rem(first + step, owners)
        forward = []
        for row in range(elements):
            running = bands_b[rows_of(row, owner), :]
            for mid in range(row):
                running = running - factor[row, mid] * forward[mid]
            forward.append(running * inverse[row])
        answer = [None] * elements
        for row in reversed(range(elements)):
            running = forward[row]
            for mid in range(row + 1, elements):
                running = running - factor[mid, row] * answer[mid]
            answer[row] = running * inverse[row]
        for pair in range(elements // 2):
            tile = jnp.concatenate([answer[2 * pair], answer[2 * pair + 1]], axis=0)
            send_b[owner, 2 * UNITS * pair : 2 * UNITS * (pair + 1), :] = tile.astype(bf16)
        send_block(send_b, recv_b, owner, b_send, b_recv)

    lane_id = lax.broadcasted_iota(jnp.int32, (cand_count, LANES), 1)
    node_id = lax.broadcasted_iota(jnp.int32, (cand_count, nodes), 1)
    eye = lax.broadcasted_iota(jnp.int32, (cand_count, cand_count), 0) == (
        lax.broadcasted_iota(jnp.int32, (cand_count, cand_count), 1)
    )
    slot_values = slot_ref[...].astype(f32)
    lane_rows = []
    for event in range(events):
        wanted = jnp.where(eye, cand_ref[event : event + 1, :].astype(f32), 0.0)
        wanted = jnp.sum(wanted, axis=1, keepdims=True)
        chosen = jnp.where(node_id.astype(f32) == wanted, slot_values, 0.0)
        lane_rows.append(jnp.sum(chosen, axis=1, keepdims=True))

    def wait_all(slots, sem):
        arrived = slots.at[pl.ds(0, groups - 1)]
        pltpu.make_async_copy(arrived, arrived, sem).wait()

    @pl.when(is_owner)
    def _():
        for slots, wide, sem, count, base in (
            (recv_a, wide_a, a_recv, events, 0),
            (recv_b, wide_b, b_recv, elements, events),
        ):
            wait_all(slots, sem)
            wide[...] = slots[...].astype(f32).reshape(wide.shape)
            stride = count * UNITS

            @pl.loop(0, UNITS)
            def _(unit):
                lanes = pl.ds(pl.multiple_of(unit * LANES, LANES), LANES)
                for row in range(count):
                    picked = wide[pl.ds(row * UNITS + unit, groups, stride=stride), :]
                    at = (base + row) * groups
                    matrix[at : at + groups, lanes] = picked.astype(bf16)

        products = lax.dot_general(
            matrix[0 : events * groups, :],
            matrix[events * groups : (events + elements) * groups, :],
            (((1,), (1,)), ((), ())),
            preferred_element_type=f32,
        )
        mixed[...] = jnp.zeros_like(mixed)
        for tile in range(elements * nodes // LANES):
            for event in range(events):
                mixed[pl.ds(tile * events + event, groups, stride=16), :] = products[
                    event * groups : (event + 1) * groups, tile * LANES : (tile + 1) * LANES
                ]
        parts_out[...] = mixed[...].astype(bf16).reshape(parts_out.shape)

        @pl.loop(1, groups)
        def _(step):
            peer = lax.rem(me + step, groups)
            pltpu.make_async_remote_copy(
                src_ref=parts_out.at[peer],
                dst_ref=parts_in.at[my_owner],
                send_sem=c_send,
                recv_sem=c_recv,
                device_id=(peer, st),
                device_id_type=MESH,
            ).start()

        parts_in[my_owner] = parts_out[me]

    @pl.when(is_owner)
    def _():
        arrived = parts_in.at[pl.ds(0, owners - 1)]
        pltpu.make_async_copy(arrived, arrived, c_recv).wait()

    @pl.when(jnp.logical_not(is_owner))
    def _():
        arrived = parts_in.at[pl.ds(0, owners)]
        pltpu.make_async_copy(arrived, arrived, c_recv).wait()

    sum_slots[st] = jnp.sum(parts_in[...].astype(f32), axis=0)

    @pl.loop(1, members)
    def _(step):
        pltpu.make_async_remote_copy(
            src_ref=sum_slots.at[st],
            dst_ref=sum_slots.at[st],
            send_sem=s_send,
            recv_sem=s_recv,
            device_id=(me, lax.rem(st + step, members)),
            device_id_type=MESH,
        ).start()

    others = sum_slots.at[pl.ds(0, members - 1)]
    pltpu.make_async_copy(others, others, s_recv).wait()
    moments = sum_slots[0]
    for member in range(1, members):
        moments = moments + sum_slots[member]

    lane_f = lane_id.astype(f32)
    out_lane = lax.broadcasted_iota(jnp.int32, (cand_count, elements), 1)
    per_tile = LANES // nodes
    for event in range(events):
        result = jnp.zeros((cand_count, elements), f32)
        for element in range(elements):
            tile, part = element // per_tile, element % per_tile
            line = moments[tile * events + event : tile * events + event + 1, :]
            mask = lane_f == lane_rows[event] + float(part * nodes)
            value = jnp.sum(jnp.where(mask, line, 0.0), axis=1, keepdims=True)
            result = jnp.where(out_lane == element, value, result)
        out_ref[event] = result

    pltpu.make_async_copy(others, others, s_send).wait()
    sent = gram_slots.at[pl.ds(0, members - 1)]
    pltpu.make_async_copy(sent, sent, gram_send).wait()

    @pl.when(is_owner)
    def _():
        for buffer, sem in ((send_a, a_send), (send_b, b_send), (parts_out, c_send)):
            sent = buffer.at[pl.ds(0, buffer.shape[0] - 1)]
            pltpu.make_async_copy(sent, sent, sem).wait()

    @pl.when(jnp.logical_not(is_owner))
    def _():
        for buffer, sem in ((send_a, a_send), (send_b, b_send)):
            pltpu.make_async_copy(buffer, buffer, sem).wait()


def shards(records, store, taper, candidates, node_slot):
    groups, members = lax.axis_size("ev"), lax.axis_size("st")
    events, stations, comps, samples = records.shape
    elements = store.shape[1]
    traces = stations * comps
    bins = 2 * taper.shape[0]
    owners = traces * bins // (UNITS * LANES)
    cand_count = candidates.shape[1]
    nodes = node_slot.shape[0]
    dims = (groups, members, events, elements, traces, owners, cand_count, nodes)
    units = traces * (bins // LANES)
    f32, bf16 = jnp.float32, jnp.bfloat16
    table = jnp.asarray(band_table(samples, taper.shape[0]))
    anywhere = pl.BlockSpec(memory_space=pl.ANY)
    vmem = pl.BlockSpec(memory_space=pltpu.VMEM)
    rows_a, rows_b = events * UNITS, elements * UNITS
    return pl.pallas_call(
        functools.partial(kernel, dims),
        out_shape=jax.ShapeDtypeStruct((events, cand_count, elements), f32),
        in_specs=[anywhere] * 3 + [vmem] * 3,
        out_specs=vmem,
        scratch_shapes=[
            pltpu.VMEM((events * traces, samples), bf16),
            pltpu.VMEM((elements * traces, samples), bf16),
            pltpu.VMEM((samples, bins), bf16),
            pltpu.VMEM((elements * traces, bins), f32),
            pltpu.VMEM((events * units, LANES), f32),
            pltpu.VMEM((elements * units, LANES), f32),
            pltpu.VMEM((owners, rows_a, LANES), bf16),
            pltpu.VMEM((owners, rows_b, LANES), bf16),
            pltpu.VMEM((groups, rows_a, LANES), bf16),
            pltpu.VMEM((groups, rows_b, LANES), bf16),
            pltpu.VMEM((groups * rows_a, LANES), f32),
            pltpu.VMEM((groups * rows_b, LANES), f32),
            pltpu.VMEM(((events + elements) * groups, UNITS * LANES), bf16),
            pltpu.VMEM((groups * 16, LANES), f32),
            pltpu.VMEM((groups, 16, LANES), bf16),
            pltpu.VMEM((owners, 16, LANES), bf16),
            pltpu.VMEM((members, 24, LANES), f32),
            pltpu.VMEM((members, 16, LANES), f32),
            pltpu.SemaphoreType.DMA((3,)),
        ]
        + [pltpu.SemaphoreType.DMA] * 10,
        compiler_params=pltpu.CompilerParams(
            collective_id=0, has_side_effects=True, vmem_limit_bytes=40 * 1024 * 1024
        ),
    )(
        records.reshape(events * traces, samples),
        store.reshape(elements * traces, samples),
        table,
        taper.reshape(1, -1),
        candidates,
        node_slot.reshape(1, -1),
    )


def solution(mesh):
    return jax.shard_map(
        shards,
        mesh=mesh,
        in_specs=(
            P("ev", "st", None, None),
            P("ev", None, "st", None, None),
            P(),
            P("ev", None),
            P(),
        ),
        out_specs=P("ev", None, None),
        check_vma=False,
    )
```

time: 426 us -> 67.7 us (0.16)
  waiting for transfers between devices: 318 us -> 0 us
  Pallas kernels: 0 us -> 64.2 us
  starting transfers between devices: 41.2 us -> 0 us
  blocking collectives: 28.6 us -> 0 us
  local copies, waits for them, and re-layouts: 16 us -> 3.28 us
  matrix products: 11.7 us -> 0 us
  other arithmetic: 7.88 us -> 0 us
    all_to_all x3 -> x0, waiting for transfers between devices: 318 us -> none  [the longest x1 304 us: shards(): lax.all_to_all(outgoing, 'ev', split_axis=0, concat_axis=0, tiled=True)]
    pallas_call x0 -> x1, Pallas kernels: none -> 64.2 us  [shards(): pl.pallas_call(functools.partial(kernel, dims), out_shape=jax.ShapeDtypeS...]
    all_to_all x3 -> x0, starting transfers between devices: 41.2 us -> none  [the longest x1 19.3 us: shards(): lax.all_to_all(slot_nodes, 'ev', split_axis=0, concat_axis=0, tiled=True)]
    psum x1 -> x0, blocking collectives: 28.6 us -> none  [shards(): proj_sum, gram_sum = lax.psum((partial_value, gram_part), 'st')]
    dot_general x5 -> x0, matrix products: 11.7 us -> none  [the longest x1 5.84 us: shards(): jnp.dot(spectra_in.reshape(leading * items, width_flat), weighted_flat.T,...]
    reshape x4 -> x2, local copies, waits for them, and re-layouts: 10.4 us -> 0.93 us  [the longest x1 0.56 us: shards(): store.reshape(elements * traces, samples)]
    another operation x1 -> x0, other arithmetic: 4.43 us -> none
  transfers between devices with their start and end apart: 3 -> 0, of which waited for: 2 -> 0; matrix products, arithmetic and copies ran while one was open for 6% -> 0% of each run, Pallas kernels for 0% -> 0%
where the time goes in v1:
time: 67.7 us; the launch traced here: 67.6 us
  Pallas kernels  64.2 us (95%)
  local copies, waits for them, and re-layouts  3.28 us (5%)
    pallas_call x1, Pallas kernels, shards(): pl.pallas_call(functools.partial(kernel, dims), out_shape=jax.ShapeDtypeS...  64.2 us
    unnamed x11, local copies, waits for them, and re-layouts  1.66 us

profile of v1, /device:TPU:1, one launch (start us, length us, event | category | flops | bytes accessed | tf_op | source)
XLA Modules:
  0.0 67.6 jit_solution(13961366895155776939)
XLA Ops:
  0.0 0.0 copy-start.4
  0.0 1.4 %copy.9 = bf16[4,18,3,1024]{3,2,1,0:T(4,128)(2,1)S(1)} copy(bf16[4,18,3,1024]{3,0,2,1:T(4,128)(2,1)} %param.6) | data formatting | bytes 884736 | tf_op args[0]
  1.4 0.0 copy-start
  1.4 0.4 reshape.12.records_hbm
  1.8 0.0 copy-done.4
  1.8 0.0 copy-start.1
  1.8 0.0 copy-start.2
  1.8 0.0 copy-start.3
  1.8 0.6 reshape.13.store_hbm
  2.4 0.2 copy-done
  2.6 0.0 copy-done.1
  2.6 0.0 copy-done.2
  2.6 0.0 copy-done.3
  2.6 64.2 %shard_map.64 = f32[4,16,6]{2,1,0:T(8,128)S(1)} custom-call(bf16[216,1024]{1,0:T(8,128)(2,1)S(1)} %reshape.12.records_hbm, bf16[324,1024]{1,0:T(8,128)(2,1)S(1)} %reshape.13.store_hbm, bf16[1024,512]{1,0:T(8,128)(2,1)S(1)} %copy-done, f32[1,256]{1,0:T(1,128)S(1)} %bitcast.2, s32[4,16]{1,0:T(4,128)S(1)} %copy-done.1, s32[1,64]{1,0:T(1,128)S(1)} %bitcast.3), custom_call_target="tpu_custom_call" | custom-call | tf_op jit(solution)/shard_map/pallas_call | solution.py:376
  66.9 0.7 %copy.10 = f32[4,16,6]{1,0,2:T(4,128)} copy(f32[4,16,6]{2,1,0:T(8,128)S(1)} %shard_map.64) | data formatting | bytes 3072 | tf_op jit(solution)/shard_map/pallas_call | solution.py:376
Async XLA Ops:
  0.0 1.8 %copy-start.4 = (bf16[1,6,18,3,1024]{4,3,2,1,0:T(4,128)(2,1)S(1)}, bf16[1,6,18,3,1024]{4,3,2,1,0:T(4,128)(2,1)}, u32[]{:S(2)}) copy-start(bf16[1,6,18,3,1024]{4,3,2,1,0:T(4,128)(2,1)} %param.7) | copy-start | bytes 1990660
  1.4 1.2 %copy-start = (bf16[1024,512]{1,0:T(8,128)(2,1)S(1)}, bf16[1024,512]{1,0:T(8,128)(2,1)}, u32[]{:S(2)}) copy-start(bf16[1024,512]{1,0:T(8,128)(2,1)} %constant.2.clone.table_hbm) | copy-start | bytes 3145732
  1.8 0.8 %copy-start.1 = (s32[4,16]{1,0:T(4,128)S(1)}, s32[4,16]{1,0:T(4,128)}, u32[]{:S(2)}) copy-start(s32[4,16]{1,0:T(4,128)} %cand_ref.1) | copy-start | bytes 772
  1.8 0.8 %copy-start.2 = (f32[256]{0:T(256)S(1)}, f32[256]{0:T(256)}, u32[]{:S(2)}) copy-start(f32[256]{0:T(256)} %param.8) | copy-start | bytes 3076
  1.8 0.8 %copy-start.3 = (s32[64]{0:T(128)S(1)}, s32[64]{0:T(128)}, u32[]{:S(2)}) copy-start(s32[64]{0:T(128)} %param.10) | copy-start | bytes 772

commit v2 on v1

--- a/solution.py
+++ b/solution.py
@@ -11,6 +11,7 @@
 
 LANES = 128
 UNITS = 8
+CHUNKS = 4
 MESH = pl.DeviceIdType.MESH
 
 
@@ -25,6 +26,22 @@
 
 def owner_chip(owner, core, owners, groups):
     return ((2 * owner + core) * groups) // (2 * owners)
+
+
+def around(step, count):
+    step = count - 1 - step
+    half = (step + 1) // 2
+    return jnp.where(lax.rem(step, 2) == 0, half, lax.rem(count - half, count))
+
+
+def far_rank(offset, count):
+    half = count // 2
+    return jnp.where(offset < half, 2 * (half - offset) - 1, 2 * (offset - half))
+
+
+def far_offset(rank, count):
+    half = count // 2
+    return jnp.where(lax.rem(rank, 2) == 0, half + rank // 2, half - (rank + 1) // 2)
 
 
 def kernel(
@@ -48,7 +65,8 @@
     recv_b,
     wide_a,
     wide_b,
-    matrix,
+    matrix_a,
+    matrix_b,
     mixed,
     parts_out,
     parts_in,
@@ -105,14 +123,22 @@
 
     loads[0].wait()
     loads[1].wait()
-    spectra[...] = jnp.dot(store_v[...], table_v[...], preferred_element_type=f32)
+    height = elements * traces
+
+    def by_tiles(values):
+        for tile in range(4):
+            start = tile * height
+            spectra[start : start + values.shape[0], :] = values[
+                :, tile * LANES : (tile + 1) * LANES
+            ]
+
+    by_tiles(jnp.dot(store_v[...], table_v[...], preferred_element_type=f32))
     for tile in range(4):
         half = (tile % 2) * LANES
         gains = taper_ref[:, half : half + LANES]
         for element in range(elements):
-            block = spectra[
-                element * traces : (element + 1) * traces, tile * LANES : (tile + 1) * LANES
-            ]
+            source = tile * height + element * traces
+            block = spectra[source : source + traces, :]
             start = element * units + tile * traces
             bands_b[start : start + traces, :] = (block * gains).astype(bf16).astype(f32)
     pair_at = {}
@@ -151,25 +177,21 @@
     samples = values.shape[1]
     mean = jnp.sum(values * values, axis=1, keepdims=True) * (1.0 / samples)
     scale = lax.rsqrt(mean + 1e-05) * (1.0 / math.sqrt(samples))
-    spectra[0 : events * traces, :] = (
-        jnp.dot(records_v[...], table_v[...], preferred_element_type=f32) * scale
-    )
+    by_tiles(jnp.dot(records_v[...], table_v[...], preferred_element_type=f32) * scale)
     for tile in range(4):
         for event in range(events):
-            block = spectra[
-                event * traces : (event + 1) * traces, tile * LANES : (tile + 1) * LANES
-            ]
+            block = spectra[pl.ds(tile * height + event, traces, stride=events), :]
             start = event * units + tile * traces
             bands_a[start : start + traces, :] = block
 
-    def send_block(buffer, slots, owner, send_sem, recv_sem):
+    def send_block(buffer, slots, owner, slot, send_sem, recv_sem):
         chip = owner_chip(owner, core, owners, groups)
 
         @pl.when(chip != me)
         def _():
             pltpu.make_async_remote_copy(
                 src_ref=buffer.at[owner],
-                dst_ref=slots.at[me],
+                dst_ref=slots.at[slot],
                 send_sem=send_sem,
                 recv_sem=recv_sem,
                 device_id=(chip, st),
@@ -178,21 +200,30 @@
 
         @pl.when(chip == me)
         def _():
-            slots[me] = buffer[owner]
+            slots[slot] = buffer[owner]
 
     def rows_of(index, owner):
         return pl.ds(pl.multiple_of(index * units + owner * UNITS, UNITS), UNITS)
 
-    @pl.loop(0, owners)
-    def _(step):
-        owner = lax.rem(first + step, owners)
+    span = groups // CHUNKS
+
+    def send_observed(step):
+        owner = lax.rem(first + around(step, owners), owners)
         for pair in range(events // 2):
             tile = jnp.concatenate(
                 [bands_a[rows_of(2 * pair, owner), :], bands_a[rows_of(2 * pair + 1, owner), :]],
                 axis=0,
             )
             send_a[owner, 2 * UNITS * pair : 2 * UNITS * (pair + 1), :] = tile.astype(bf16)
-        send_block(send_a, recv_a, owner, a_send, a_recv)
+        offset = lax.rem(owner_chip(owner, core, owners, groups) - me + groups, groups)
+        rank = far_rank(offset, groups)
+        send_block(send_a, recv_a, owner, rank, a_send, a_recv.at[rank // span])
+
+    early = owners // 2
+
+    @pl.loop(0, early)
+    def _(step):
+        send_observed(step)
 
     others = gram_slots.at[pl.ds(0, members - 1)]
     pltpu.make_async_copy(others, others, gram_recv).wait()
@@ -218,7 +249,7 @@
 
     @pl.loop(0, owners)
     def _(step):
-        owner = lax.rem(first + step, owners)
+        owner = lax.rem(first + around(step, owners), owners)
         forward = []
         for row in range(elements):
             running = bands_b[rows_of(row, owner), :]
@@ -234,7 +265,11 @@
         for pair in range(elements // 2):
             tile = jnp.concatenate([answer[2 * pair], answer[2 * pair + 1]], axis=0)
             send_b[owner, 2 * UNITS * pair : 2 * UNITS * (pair + 1), :] = tile.astype(bf16)
-        send_block(send_b, recv_b, owner, b_send, b_recv)
+        send_block(send_b, recv_b, owner, me, b_send, b_recv)
+
+    @pl.loop(early, owners)
+    def _(step):
+        send_observed(step)
 
     lane_id = lax.broadcasted_iota(jnp.int32, (cand_count, LANES), 1)
     node_id = lax.broadcasted_iota(jnp.int32, (cand_count, nodes), 1)
@@ -249,55 +284,54 @@
         chosen = jnp.where(node_id.astype(f32) == wanted, slot_values, 0.0)
         lane_rows.append(jnp.sum(chosen, axis=1, keepdims=True))
 
-    def wait_all(slots, sem):
-        arrived = slots.at[pl.ds(0, groups - 1)]
-        pltpu.make_async_copy(arrived, arrived, sem).wait()
+    def spread(wide, target, count, height):
+        @pl.loop(0, UNITS)
+        def _(unit):
+            lanes = pl.ds(pl.multiple_of(unit * LANES, LANES), LANES)
+            for row in range(count):
+                picked = wide[pl.ds(row * UNITS + unit, height, stride=count * UNITS), :]
+                target[row * height : (row + 1) * height, lanes] = picked.astype(bf16)
 
     @pl.when(is_owner)
     def _():
-        for slots, wide, sem, count, base in (
-            (recv_a, wide_a, a_recv, events, 0),
-            (recv_b, wide_b, b_recv, elements, events),
-        ):
-            wait_all(slots, sem)
-            wide[...] = slots[...].astype(f32).reshape(wide.shape)
-            stride = count * UNITS
-
-            @pl.loop(0, UNITS)
-            def _(unit):
-                lanes = pl.ds(pl.multiple_of(unit * LANES, LANES), LANES)
-                for row in range(count):
-                    picked = wide[pl.ds(row * UNITS + unit, groups, stride=stride), :]
-                    at = (base + row) * groups
-                    matrix[at : at + groups, lanes] = picked.astype(bf16)
-
-        products = lax.dot_general(
-            matrix[0 : events * groups, :],
-            matrix[events * groups : (events + elements) * groups, :],
-            (((1,), (1,)), ((), ())),
-            preferred_element_type=f32,
-        )
         mixed[...] = jnp.zeros_like(mixed)
-        for tile in range(elements * nodes // LANES):
-            for event in range(events):
-                mixed[pl.ds(tile * events + event, groups, stride=16), :] = products[
-                    event * groups : (event + 1) * groups, tile * LANES : (tile + 1) * LANES
-                ]
-        parts_out[...] = mixed[...].astype(bf16).reshape(parts_out.shape)
-
-        @pl.loop(1, groups)
-        def _(step):
-            peer = lax.rem(me + step, groups)
-            pltpu.make_async_remote_copy(
-                src_ref=parts_out.at[peer],
-                dst_ref=parts_in.at[my_owner],
-                send_sem=c_send,
-                recv_sem=c_recv,
-                device_id=(peer, st),
-                device_id_type=MESH,
-            ).start()
-
-        parts_in[my_owner] = parts_out[me]
+        arrived = recv_b.at[pl.ds(0, groups - 1)]
+        pltpu.make_async_copy(arrived, arrived, b_recv).wait()
+        wide_b[...] = recv_b[...].astype(f32).reshape(wide_b.shape)
+        spread(wide_b, matrix_b, elements, groups)
+        for chunk in range(CHUNKS):
+            start, stop = chunk * span, (chunk + 1) * span
+            remote = min(stop, groups - 1)
+            arrived = recv_a.at[pl.ds(start, remote - start)]
+            pltpu.make_async_copy(arrived, arrived, a_recv.at[chunk]).wait()
+            wide_a[...] = recv_a[start:stop].astype(f32).reshape(wide_a.shape)
+            spread(wide_a, matrix_a, events, span)
+            products = lax.dot_general(
+                matrix_a[...],
+                matrix_b[...],
+                (((1,), (1,)), ((), ())),
+                preferred_element_type=f32,
+            )
+            for tile in range(elements * nodes // LANES):
+                for event in range(events):
+                    mixed[pl.ds(tile * events + event, span, stride=16), :] = products[
+                        event * span : (event + 1) * span, tile * LANES : (tile + 1) * LANES
+                    ]
+            parts_out[start:stop] = mixed[...].astype(bf16).reshape(span, 16, LANES)
+
+            @pl.loop(start, remote)
+            def _(rank):
+                peer = lax.rem(me - far_offset(rank, groups) + groups, groups)
+                pltpu.make_async_remote_copy(
+                    src_ref=parts_out.at[rank],
+                    dst_ref=parts_in.at[my_owner],
+                    send_sem=c_send,
+                    recv_sem=c_recv,
+                    device_id=(peer, st),
+                    device_id_type=MESH,
+                ).start()
+
+        parts_in[my_owner] = parts_out[groups - 1]
 
     @pl.when(is_owner)
     def _():
@@ -382,29 +416,32 @@
             pltpu.VMEM((events * traces, samples), bf16),
             pltpu.VMEM((elements * traces, samples), bf16),
             pltpu.VMEM((samples, bins), bf16),
-            pltpu.VMEM((elements * traces, bins), f32),
+            pltpu.VMEM((elements * traces * (bins // LANES), LANES), f32),
             pltpu.VMEM((events * units, LANES), f32),
             pltpu.VMEM((elements * units, LANES), f32),
             pltpu.VMEM((owners, rows_a, LANES), bf16),
             pltpu.VMEM((owners, rows_b, LANES), bf16),
             pltpu.VMEM((groups, rows_a, LANES), bf16),
             pltpu.VMEM((groups, rows_b, LANES), bf16),
-            pltpu.VMEM((groups * rows_a, LANES), f32),
+            pltpu.VMEM((groups // CHUNKS * rows_a, LANES), f32),
             pltpu.VMEM((groups * rows_b, LANES), f32),
-            pltpu.VMEM(((events + elements) * groups, UNITS * LANES), bf16),
-            pltpu.VMEM((groups * 16, LANES), f32),
+            pltpu.VMEM((groups // CHUNKS * events, UNITS * LANES), bf16),
+            pltpu.VMEM((elements * groups, UNITS * LANES), bf16),
+            pltpu.VMEM((groups // CHUNKS * 16, LANES), f32),
             pltpu.VMEM((groups, 16, LANES), bf16),
             pltpu.VMEM((owners, 16, LANES), bf16),
             pltpu.VMEM((members, 24, LANES), f32),
             pltpu.VMEM((members, 16, LANES), f32),
             pltpu.SemaphoreType.DMA((3,)),
         ]
-        + [pltpu.SemaphoreType.DMA] * 10,
+        + [pltpu.SemaphoreType.DMA] * 3
+        + [pltpu.SemaphoreType.DMA((CHUNKS,))]
+        + [pltpu.SemaphoreType.DMA] * 6,
         compiler_params=pltpu.CompilerParams(
             collective_id=0, has_side_effects=True, vmem_limit_bytes=40 * 1024 * 1024
         ),
     )(
-        records.reshape(events * traces, samples),
+        records.transpose(1, 2, 0, 3).reshape(traces * events, samples),
         store.reshape(elements * traces, samples),
         table,
         taper.reshape(1, -1),

time: 67.7 us -> 64 us (0.945)
  Pallas kernels: 64.2 us -> 61 us
    pallas_call x1, Pallas kernels: 64.2 us -> 61 us  [shards(): pl.pallas_call(functools.partial(kernel, dims), out_shape=jax.ShapeDtypeS...]
    unnamed x11 -> x10, local copies, waits for them, and re-layouts: 1.66 us -> 0.25 us
    reshape x1, local copies, waits for them, and re-layouts: 0.37 us -> 1.25 us  [shards(): records.transpose(1, 2, 0, 3).reshape(traces * events, samples)]
where the time goes in v2:
time: 64 us; the launch traced here: 63.8 us
  Pallas kernels  61 us (95%)
  local copies, waits for them, and re-layouts  2.75 us (4%)
    pallas_call x1, Pallas kernels, shards(): pl.pallas_call(functools.partial(kernel, dims), out_shape=jax.ShapeDtypeS...  61 us

profile of v2, /device:TPU:1, one launch (start us, length us, event | category | flops | bytes accessed | tf_op | source)
XLA Modules:
  0.0 63.8 jit_solution(9818901154389729254)
XLA Ops:
  0.0 0.0 copy-start.4
  0.0 0.0 copy-start
  0.0 1.3 %reshape.12.records_hbm = bf16[216,1024]{1,0:T(8,128)(2,1)S(1)} reshape(bf16[18,3,4,1024]{3,2,1,0:T(4,128)(2,1)} %bitcast.5) | data formatting | bytes 884736 | tf_op jit(solution)/shard_map/reshape | solution.py:444
  1.3 0.0 copy-done.4
  1.3 0.0 copy-start.1
  1.3 0.0 copy-start.2
  1.3 0.0 copy-start.3
  1.3 0.6 reshape.13.store_hbm
  1.9 0.0 copy-done
  1.9 0.2 copy-done.1
  2.1 0.0 copy-done.2
  2.1 0.0 copy-done.3
  2.1 61.0 %shard_map.64 = f32[4,16,6]{2,1,0:T(8,128)S(1)} custom-call(bf16[216,1024]{1,0:T(8,128)(2,1)S(1)} %reshape.12.records_hbm, bf16[324,1024]{1,0:T(8,128)(2,1)S(1)} %reshape.13.store_hbm, bf16[1024,512]{1,0:T(8,128)(2,1)S(1)} %copy-done, f32[1,256]{1,0:T(1,128)S(1)} %bitcast.3, s32[4,16]{1,0:T(4,128)S(1)} %copy-done.1, s32[1,64]{1,0:T(1,128)S(1)} %bitcast.4), custom_call_target="tpu_custom_call" | custom-call | tf_op jit(solution)/shard_map/pallas_call | solution.py:410
  63.1 0.7 %copy.8 = f32[4,16,6]{1,0,2:T(4,128)} copy(f32[4,16,6]{2,1,0:T(8,128)S(1)} %shard_map.64) | data formatting | bytes 3072 | tf_op jit(solution)/shard_map/pallas_call | solution.py:410
Async XLA Ops:
  0.0 1.3 %copy-start.4 = (bf16[1,6,18,3,1024]{4,3,2,1,0:T(4,128)(2,1)S(1)}, bf16[1,6,18,3,1024]{4,3,2,1,0:T(4,128)(2,1)}, u32[]{:S(2)}) copy-start(bf16[1,6,18,3,1024]{4,3,2,1,0:T(4,128)(2,1)} %param.7) | copy-start | bytes 1990660
  0.0 1.9 %copy-start = (bf16[1024,512]{1,0:T(8,128)(2,1)S(1)}, bf16[1024,512]{1,0:T(8,128)(2,1)}, u32[]{:S(2)}) copy-start(bf16[1024,512]{1,0:T(8,128)(2,1)} %constant.2.clone.table_hbm) | copy-start | bytes 3145732
  1.3 0.8 %copy-start.1 = (s32[4,16]{1,0:T(4,128)S(1)}, s32[4,16]{1,0:T(4,128)}, u32[]{:S(2)}) copy-start(s32[4,16]{1,0:T(4,128)} %cand_ref.1) | copy-start | bytes 772
  1.3 0.8 %copy-start.2 = (f32[256]{0:T(256)S(1)}, f32[256]{0:T(256)}, u32[]{:S(2)}) copy-start(f32[256]{0:T(256)} %param.8) | copy-start | bytes 3076
  1.3 0.8 %copy-start.3 = (s32[64]{0:T(128)S(1)}, s32[64]{0:T(128)}, u32[]{:S(2)}) copy-start(s32[64]{0:T(128)} %param.10) | copy-start | bytes 772

commit v3 on v2

--- a/solution.py
+++ b/solution.py
@@ -49,13 +49,16 @@
     records_hbm,
     store_hbm,
     table_hbm,
-    taper_ref,
-    cand_ref,
-    slot_ref,
+    taper_hbm,
+    cand_hbm,
+    slot_hbm,
     out_ref,
     records_v,
     store_v,
     table_v,
+    taper_ref,
+    cand_ref,
+    slot_ref,
     spectra,
     bands_a,
     bands_b,
@@ -96,21 +99,25 @@
         pltpu.make_async_copy(table_hbm, table_v, load_sem.at[0]),
         pltpu.make_async_copy(store_hbm, store_v, load_sem.at[1]),
         pltpu.make_async_copy(records_hbm, records_v, load_sem.at[2]),
+        pltpu.make_async_copy(taper_hbm, taper_ref, load_sem.at[3]),
+        pltpu.make_async_copy(cand_hbm, cand_ref, load_sem.at[4]),
+        pltpu.make_async_copy(slot_hbm, slot_ref, load_sem.at[5]),
     ]
     for load in loads:
         load.start()
 
     barrier = pltpu.get_barrier_semaphore()
 
-    @pl.loop(1, members)
-    def _(step):
-        peer = lax.rem(st + step, members)
+    def shifted(index, offset, count):
+        total = index + offset
+        return jnp.where(total >= count, total - count, total)
+
+    for offset in sorted(range(1, groups), key=lambda at: abs(at - groups // 2)):
+        peer = shifted(me, offset, groups)
+        pl.semaphore_signal(barrier, inc=1, device_id=(peer, st), device_id_type=MESH)
+    for offset in range(1, members):
+        peer = shifted(st, offset, members)
         pl.semaphore_signal(barrier, inc=1, device_id=(me, peer), device_id_type=MESH)
-
-    @pl.loop(1, groups)
-    def _(step):
-        peer = lax.rem(me + step, groups)
-        pl.semaphore_signal(barrier, inc=1, device_id=(peer, st), device_id_type=MESH)
 
     ranked = (2 * owners * me + groups - 1) // groups
     is_owner = (
@@ -123,6 +130,7 @@
 
     loads[0].wait()
     loads[1].wait()
+    loads[3].wait()
     height = elements * traces
 
     def by_tiles(values):
@@ -132,7 +140,9 @@
                 :, tile * LANES : (tile + 1) * LANES
             ]
 
-    by_tiles(jnp.dot(store_v[...], table_v[...], preferred_element_type=f32))
+    samples = table_v.shape[0]
+    rows = store_v[...].reshape(elements * traces, samples)
+    by_tiles(jnp.dot(rows, table_v[...], preferred_element_type=f32))
     for tile in range(4):
         half = (tile % 2) * LANES
         gains = taper_ref[:, half : half + LANES]
@@ -156,6 +166,30 @@
     shares.append(jnp.zeros((gram_rows - len(shares), LANES), f32))
     gram_slots[st] = jnp.concatenate(shares, axis=0)
 
+    loads[2].wait()
+    rows = records_v[...].reshape(traces * events, samples)
+    values = rows.astype(f32)
+    mean = jnp.sum(values * values, axis=1, keepdims=True) * (1.0 / samples)
+    scale = lax.rsqrt(mean + 1e-05) * (1.0 / math.sqrt(samples))
+    by_tiles(jnp.dot(rows, table_v[...], preferred_element_type=f32) * scale)
+    for tile in range(4):
+        for event in range(events):
+            block = spectra[pl.ds(tile * height + event, traces, stride=events), :]
+            start = event * units + tile * traces
+            bands_a[start : start + traces, :] = block
+
+    def rows_of(index, owner):
+        return pl.ds(pl.multiple_of(index * units + owner * UNITS, UNITS), UNITS)
+
+    @pl.loop(0, owners)
+    def _(owner):
+        for pair in range(events // 2):
+            tile = jnp.concatenate(
+                [bands_a[rows_of(2 * pair, owner), :], bands_a[rows_of(2 * pair + 1, owner), :]],
+                axis=0,
+            )
+            send_a[owner, 2 * UNITS * pair : 2 * UNITS * (pair + 1), :] = tile.astype(bf16)
+
     pl.semaphore_wait(barrier, groups + members - 2)
 
     def gram_copy(step):
@@ -171,18 +205,6 @@
     @pl.loop(1, members)
     def _(step):
         gram_copy(step).start()
-
-    loads[2].wait()
-    values = records_v[...].astype(f32)
-    samples = values.shape[1]
-    mean = jnp.sum(values * values, axis=1, keepdims=True) * (1.0 / samples)
-    scale = lax.rsqrt(mean + 1e-05) * (1.0 / math.sqrt(samples))
-    by_tiles(jnp.dot(records_v[...], table_v[...], preferred_element_type=f32) * scale)
-    for tile in range(4):
-        for event in range(events):
-            block = spectra[pl.ds(tile * height + event, traces, stride=events), :]
-            start = event * units + tile * traces
-            bands_a[start : start + traces, :] = block
 
     def send_block(buffer, slots, owner, slot, send_sem, recv_sem):
         chip = owner_chip(owner, core, owners, groups)
@@ -202,19 +224,10 @@
         def _():
             slots[slot] = buffer[owner]
 
-    def rows_of(index, owner):
-        return pl.ds(pl.multiple_of(index * units + owner * UNITS, UNITS), UNITS)
-
     span = groups // CHUNKS
 
     def send_observed(step):
         owner = lax.rem(first + around(step, owners), owners)
-        for pair in range(events // 2):
-            tile = jnp.concatenate(
-                [bands_a[rows_of(2 * pair, owner), :], bands_a[rows_of(2 * pair + 1, owner), :]],
-                axis=0,
-            )
-            send_a[owner, 2 * UNITS * pair : 2 * UNITS * (pair + 1), :] = tile.astype(bf16)
         offset = lax.rem(owner_chip(owner, core, owners, groups) - me + groups, groups)
         rank = far_rank(offset, groups)
         send_block(send_a, recv_a, owner, rank, a_send, a_recv.at[rank // span])
@@ -271,6 +284,8 @@
     def _(step):
         send_observed(step)
 
+    loads[4].wait()
+    loads[5].wait()
     lane_id = lax.broadcasted_iota(jnp.int32, (cand_count, LANES), 1)
     node_id = lax.broadcasted_iota(jnp.int32, (cand_count, nodes), 1)
     eye = lax.broadcasted_iota(jnp.int32, (cand_count, cand_count), 0) == (
@@ -363,17 +378,20 @@
         moments = moments + sum_slots[member]
 
     lane_f = lane_id.astype(f32)
-    out_lane = lax.broadcasted_iota(jnp.int32, (cand_count, elements), 1)
+    out_lane = lax.broadcasted_iota(jnp.int32, (cand_count, LANES), 1)
     per_tile = LANES // nodes
+    result = jnp.zeros((cand_count, LANES), f32)
     for event in range(events):
-        result = jnp.zeros((cand_count, elements), f32)
         for element in range(elements):
             tile, part = element // per_tile, element % per_tile
             line = moments[tile * events + event : tile * events + event + 1, :]
             mask = lane_f == lane_rows[event] + float(part * nodes)
             value = jnp.sum(jnp.where(mask, line, 0.0), axis=1, keepdims=True)
-            result = jnp.where(out_lane == element, value, result)
-        out_ref[event] = result
+            result = jnp.where(out_lane == element * events + event, value, result)
+    result = jnp.concatenate([result, jnp.zeros((LANES - cand_count, LANES), f32)], axis=0).T
+    for element in range(elements):
+        rows = result[element * events : (element + 1) * events, :cand_count]
+        out_ref[element] = rows
 
     pltpu.make_async_copy(others, others, s_send).wait()
     sent = gram_slots.at[pl.ds(0, members - 1)]
@@ -404,18 +422,19 @@
     units = traces * (bins // LANES)
     f32, bf16 = jnp.float32, jnp.bfloat16
     table = jnp.asarray(band_table(samples, taper.shape[0]))
-    anywhere = pl.BlockSpec(memory_space=pl.ANY)
-    vmem = pl.BlockSpec(memory_space=pltpu.VMEM)
     rows_a, rows_b = events * UNITS, elements * UNITS
-    return pl.pallas_call(
+    result = pl.pallas_call(
         functools.partial(kernel, dims),
-        out_shape=jax.ShapeDtypeStruct((events, cand_count, elements), f32),
-        in_specs=[anywhere] * 3 + [vmem] * 3,
-        out_specs=vmem,
+        out_shape=jax.ShapeDtypeStruct((elements, events, cand_count), f32),
+        in_specs=[pl.BlockSpec(memory_space=pltpu.HBM)] * 6,
+        out_specs=pl.BlockSpec(memory_space=pltpu.VMEM),
         scratch_shapes=[
-            pltpu.VMEM((events * traces, samples), bf16),
-            pltpu.VMEM((elements * traces, samples), bf16),
+            pltpu.VMEM((traces, events, samples), bf16),
+            pltpu.VMEM((elements * stations, comps, samples), bf16),
             pltpu.VMEM((samples, bins), bf16),
+            pltpu.VMEM((1, taper.shape[0]), f32),
+            pltpu.VMEM((events, cand_count), jnp.int32),
+            pltpu.VMEM((1, nodes), jnp.int32),
             pltpu.VMEM((elements * traces * (bins // LANES), LANES), f32),
             pltpu.VMEM((events * units, LANES), f32),
             pltpu.VMEM((elements * units, LANES), f32),
@@ -432,22 +451,23 @@
             pltpu.VMEM((owners, 16, LANES), bf16),
             pltpu.VMEM((members, 24, LANES), f32),
             pltpu.VMEM((members, 16, LANES), f32),
-            pltpu.SemaphoreType.DMA((3,)),
+            pltpu.SemaphoreType.DMA((6,)),
         ]
         + [pltpu.SemaphoreType.DMA] * 3
         + [pltpu.SemaphoreType.DMA((CHUNKS,))]
         + [pltpu.SemaphoreType.DMA] * 6,
         compiler_params=pltpu.CompilerParams(
-            collective_id=0, has_side_effects=True, vmem_limit_bytes=40 * 1024 * 1024
+            collective_id=0, has_side_effects=True, vmem_limit_bytes=215 * 256 * 1024
         ),
     )(
-        records.transpose(1, 2, 0, 3).reshape(traces * events, samples),
-        store.reshape(elements * traces, samples),
+        records.transpose(1, 2, 0, 3).reshape(traces, events, samples),
+        store.reshape(elements * stations, comps, samples),
         table,
         taper.reshape(1, -1),
         candidates,
         node_slot.reshape(1, -1),
     )
+    return result.transpose(1, 2, 0)
 
 
 def solution(mesh):

time: 64 us -> 61.3 us (0.958)
  local copies, waits for them, and re-layouts: 2.75 us -> 1.29 us
  Pallas kernels: 61 us -> 59.8 us
    reshape x2 -> x0, local copies, waits for them, and re-layouts: 1.81 us -> none  [the longest x1 1.25 us: shards(): records.transpose(1, 2, 0, 3).reshape(traces * events, samples)]
    pallas_call x1, Pallas kernels: 61 us -> 59.8 us  [shards(): pl.pallas_call(functools.partial(kernel, dims), out_shape=jax.ShapeDtypeS...]
    unnamed x10 -> x7, local copies, waits for them, and re-layouts: 0.25 us -> 1.29 us
    pallas_call x1 -> x0, local copies, waits for them, and re-layouts: 0.69 us -> none  [shards(): pl.pallas_call(functools.partial(kernel, dims), out_shape=jax.ShapeDtypeS...]
where the time goes in v3:
time: 61.3 us; the launch traced here: 61.1 us
  Pallas kernels  59.8 us (98%)
  local copies, waits for them, and re-layouts  1.29 us (2%)
    pallas_call x1, Pallas kernels, shards(): pl.pallas_call(functools.partial(kernel, dims), out_shape=jax.ShapeDtypeS...  59.8 us
    unnamed x7, local copies, waits for them, and re-layouts  1.29 us

profile of v3, /device:TPU:1, one launch (start us, length us, event | category | flops | bytes accessed | tf_op | source)
XLA Modules:
  0.0 61.1 jit_solution(18259766800391043958)
XLA Ops:
  0.0 0.0 copy-start
  0.0 0.0 copy-start.1
  0.0 0.0 copy-start.2
  0.0 0.7 %copy-done = s32[4,16]{1,0:T(4,128)S(1)} copy-done((s32[4,16]{1,0:T(4,128)S(1)}, s32[4,16]{1,0:T(4,128)}, u32[]{:S(2)}) %copy-start) | copy-done | bytes 280
  0.7 0.0 copy-done.1
  0.7 0.0 copy-done.2
  0.7 59.8 %shard_map.64 = f32[6,4,16]{2,1,0:T(4,128)S(1)} custom-call(bf16[54,4,1024]{2,1,0:T(4,128)(2,1)} %bitcast.11, bf16[108,3,1024]{2,1,0:T(4,128)(2,1)} %bitcast.10, bf16[1024,512]{1,0:T(8,128)(2,1)} %constant.2.clone.table_hbm, f32[1,256]{1,0:T(1,128)S(1)} %bitcast.8, s32[4,16]{1,0:T(4,128)S(1)} %copy-done, s32[1,64]{1,0:T(1,128)S(1)} %bitcast.9), custom_call_target="tpu_custom_call" | custom-call | tf_op jit(solution)/shard_map/pallas_call | solution.py:426
  60.5 0.6 copy.8
Async XLA Ops:
  0.0 0.7 %copy-start = (s32[4,16]{1,0:T(4,128)S(1)}, s32[4,16]{1,0:T(4,128)}, u32[]{:S(2)}) copy-start(s32[4,16]{1,0:T(4,128)} %cand_hbm.1) | copy-start | bytes 772
  0.0 0.7 %copy-start.1 = (f32[256]{0:T(256)S(1)}, f32[256]{0:T(256)}, u32[]{:S(2)}) copy-start(f32[256]{0:T(256)} %param.8) | copy-start | bytes 3076
  0.0 0.7 %copy-start.2 = (s32[64]{0:T(128)S(1)}, s32[64]{0:T(128)}, u32[]{:S(2)}) copy-start(s32[64]{0:T(128)} %param.10) | copy-start | bytes 772

commit v4 on v3

--- a/solution.py
+++ b/solution.py
@@ -115,7 +115,8 @@
     for offset in sorted(range(1, groups), key=lambda at: abs(at - groups // 2)):
         peer = shifted(me, offset, groups)
         pl.semaphore_signal(barrier, inc=1, device_id=(peer, st), device_id_type=MESH)
-    for offset in range(1, members):
+    far_members = sorted(range(1, members), key=lambda at: abs(at - members // 2))
+    for offset in far_members:
         peer = shifted(st, offset, members)
         pl.semaphore_signal(barrier, inc=1, device_id=(me, peer), device_id_type=MESH)
 
@@ -198,12 +199,11 @@
             dst_ref=gram_slots.at[st],
             send_sem=gram_send,
             recv_sem=gram_recv,
-            device_id=(me, lax.rem(st + step, members)),
+            device_id=(me, shifted(st, step, members)),
             device_id_type=MESH,
         )
 
-    @pl.loop(1, members)
-    def _(step):
+    for step in far_members:
         gram_copy(step).start()
 
     def send_block(buffer, slots, owner, slot, send_sem, recv_sem):
@@ -360,14 +360,13 @@
 
     sum_slots[st] = jnp.sum(parts_in[...].astype(f32), axis=0)
 
-    @pl.loop(1, members)
-    def _(step):
+    for step in far_members:
         pltpu.make_async_remote_copy(
             src_ref=sum_slots.at[st],
             dst_ref=sum_slots.at[st],
             send_sem=s_send,
             recv_sem=s_recv,
-            device_id=(me, lax.rem(st + step, members)),
+            device_id=(me, shifted(st, step, members)),
             device_id_type=MESH,
         ).start()
 

time: 61.3 us -> 61 us (level)
  no operation moved by 1% of the time
where the time goes in v4:
time: 61 us; the launch traced here: 60.8 us
  Pallas kernels  59.5 us (98%)
  local copies, waits for them, and re-layouts  1.29 us (2%)
    pallas_call x1, Pallas kernels, shards(): pl.pallas_call(functools.partial(kernel, dims), out_shape=jax.ShapeDtypeS...  59.5 us
    unnamed x7, local copies, waits for them, and re-layouts  1.29 us

profile of v4, /device:TPU:1, one launch (start us, length us, event | category | flops | bytes accessed | tf_op | source)
XLA Modules:
  0.0 60.8 jit_solution(4371026155678948518)
XLA Ops:
  0.0 0.0 copy-start
  0.0 0.0 copy-start.1
  0.0 0.0 copy-start.2
  0.0 0.7 %copy-done = s32[4,16]{1,0:T(4,128)S(1)} copy-done((s32[4,16]{1,0:T(4,128)S(1)}, s32[4,16]{1,0:T(4,128)}, u32[]{:S(2)}) %copy-start) | copy-done | bytes 280
  0.7 0.0 copy-done.1
  0.7 0.0 copy-done.2
  0.7 59.5 %shard_map.64 = f32[6,4,16]{2,1,0:T(4,128)S(1)} custom-call(bf16[54,4,1024]{2,1,0:T(4,128)(2,1)} %bitcast.11, bf16[108,3,1024]{2,1,0:T(4,128)(2,1)} %bitcast.10, bf16[1024,512]{1,0:T(8,128)(2,1)} %constant.2.clone.table_hbm, f32[1,256]{1,0:T(1,128)S(1)} %bitcast.8, s32[4,16]{1,0:T(4,128)S(1)} %copy-done, s32[1,64]{1,0:T(1,128)S(1)} %bitcast.9), custom_call_target="tpu_custom_call" | custom-call | tf_op jit(solution)/shard_map/pallas_call | solution.py:425
  60.2 0.6 copy.8
Async XLA Ops:
  0.0 0.7 %copy-start = (s32[4,16]{1,0:T(4,128)S(1)}, s32[4,16]{1,0:T(4,128)}, u32[]{:S(2)}) copy-start(s32[4,16]{1,0:T(4,128)} %cand_hbm.1) | copy-start | bytes 772
  0.0 0.7 %copy-start.1 = (f32[256]{0:T(256)S(1)}, f32[256]{0:T(256)}, u32[]{:S(2)}) copy-start(f32[256]{0:T(256)} %param.8) | copy-start | bytes 3076
  0.0 0.7 %copy-start.2 = (s32[64]{0:T(128)S(1)}, s32[64]{0:T(128)}, u32[]{:S(2)}) copy-start(s32[64]{0:T(128)} %param.10) | copy-start | bytes 772

commit v5 on v4

--- a/solution.py
+++ b/solution.py
@@ -312,14 +312,18 @@
         mixed[...] = jnp.zeros_like(mixed)
         arrived = recv_b.at[pl.ds(0, groups - 1)]
         pltpu.make_async_copy(arrived, arrived, b_recv).wait()
-        wide_b[...] = recv_b[...].astype(f32).reshape(wide_b.shape)
+        wide_b[0 : groups * elements * UNITS, :] = (
+            recv_b[...].astype(f32).reshape(groups * elements * UNITS, LANES)
+        )
         spread(wide_b, matrix_b, elements, groups)
         for chunk in range(CHUNKS):
             start, stop = chunk * span, (chunk + 1) * span
             remote = min(stop, groups - 1)
             arrived = recv_a.at[pl.ds(start, remote - start)]
             pltpu.make_async_copy(arrived, arrived, a_recv.at[chunk]).wait()
-            wide_a[...] = recv_a[start:stop].astype(f32).reshape(wide_a.shape)
+            wide_a[0 : span * events * UNITS, :] = (
+                recv_a[start:stop].astype(f32).reshape(span * events * UNITS, LANES)
+            )
             spread(wide_a, matrix_a, events, span)
             products = lax.dot_general(
                 matrix_a[...],
@@ -332,7 +336,9 @@
                     mixed[pl.ds(tile * events + event, span, stride=16), :] = products[
                         event * span : (event + 1) * span, tile * LANES : (tile + 1) * LANES
                     ]
-            parts_out[start:stop] = mixed[...].astype(bf16).reshape(span, 16, LANES)
+            parts_out[start:stop] = (
+                mixed[0 : span * 16, :].astype(bf16).reshape(span, 16, LANES)
+            )
 
             @pl.loop(start, remote)
             def _(rank):
@@ -441,11 +447,11 @@
             pltpu.VMEM((owners, rows_b, LANES), bf16),
             pltpu.VMEM((groups, rows_a, LANES), bf16),
             pltpu.VMEM((groups, rows_b, LANES), bf16),
-            pltpu.VMEM((groups // CHUNKS * rows_a, LANES), f32),
-            pltpu.VMEM((groups * rows_b, LANES), f32),
+            pltpu.VMEM(((groups // CHUNKS + 1) * rows_a, LANES), f32),
+            pltpu.VMEM(((groups + 1) * rows_b, LANES), f32),
             pltpu.VMEM((groups // CHUNKS * events, UNITS * LANES), bf16),
             pltpu.VMEM((elements * groups, UNITS * LANES), bf16),
-            pltpu.VMEM((groups // CHUNKS * 16, LANES), f32),
+            pltpu.VMEM(((groups // CHUNKS + 1) * 16, LANES), f32),
             pltpu.VMEM((groups, 16, LANES), bf16),
             pltpu.VMEM((owners, 16, LANES), bf16),
             pltpu.VMEM((members, 24, LANES), f32),

time: 61 us -> 61 us (level)
  no operation moved by 1% of the time
where the time goes in v5:
time: 61 us; the launch traced here: 60.8 us
  Pallas kernels  59.5 us (98%)
  local copies, waits for them, and re-layouts  1.29 us (2%)
    pallas_call x1, Pallas kernels, shards(): pl.pallas_call(functools.partial(kernel, dims), out_shape=jax.ShapeDtypeS...  59.5 us
    unnamed x7, local copies, waits for them, and re-layouts  1.29 us

profile of v5, /device:TPU:1, one launch (start us, length us, event | category | flops | bytes accessed | tf_op | source)
XLA Modules:
  0.0 60.8 jit_solution(5956124099375818043)
XLA Ops:
  0.0 0.0 copy-start
  0.0 0.0 copy-start.1
  0.0 0.0 copy-start.2
  0.0 0.7 %copy-done = s32[4,16]{1,0:T(4,128)S(1)} copy-done((s32[4,16]{1,0:T(4,128)S(1)}, s32[4,16]{1,0:T(4,128)}, u32[]{:S(2)}) %copy-start) | copy-done | bytes 280
  0.7 0.0 copy-done.1
  0.7 0.0 copy-done.2
  0.7 59.5 %shard_map.64 = f32[6,4,16]{2,1,0:T(4,128)S(1)} custom-call(bf16[54,4,1024]{2,1,0:T(4,128)(2,1)} %bitcast.11, bf16[108,3,1024]{2,1,0:T(4,128)(2,1)} %bitcast.10, bf16[1024,512]{1,0:T(8,128)(2,1)} %constant.2.clone.table_hbm, f32[1,256]{1,0:T(1,128)S(1)} %bitcast.8, s32[4,16]{1,0:T(4,128)S(1)} %copy-done, s32[1,64]{1,0:T(1,128)S(1)} %bitcast.9), custom_call_target="tpu_custom_call" | custom-call | tf_op jit(solution)/shard_map/pallas_call | solution.py:431
  60.2 0.6 copy.8
Async XLA Ops:
  0.0 0.7 %copy-start = (s32[4,16]{1,0:T(4,128)S(1)}, s32[4,16]{1,0:T(4,128)}, u32[]{:S(2)}) copy-start(s32[4,16]{1,0:T(4,128)} %cand_hbm.1) | copy-start | bytes 772
  0.0 0.7 %copy-start.1 = (f32[256]{0:T(256)S(1)}, f32[256]{0:T(256)}, u32[]{:S(2)}) copy-start(f32[256]{0:T(256)} %param.8) | copy-start | bytes 3076
  0.0 0.7 %copy-start.2 = (s32[64]{0:T(128)S(1)}, s32[64]{0:T(128)}, u32[]{:S(2)}) copy-start(s32[64]{0:T(128)} %param.10) | copy-start | bytes 772

commit v6 on v5

--- a/solution.py
+++ b/solution.py
@@ -430,7 +430,7 @@
     rows_a, rows_b = events * UNITS, elements * UNITS
     result = pl.pallas_call(
         functools.partial(kernel, dims),
-        out_shape=jax.ShapeDtypeStruct((elements, events, cand_count), f32),
+        out_shape=pltpu.VMEM((elements, events, cand_count), f32),
         in_specs=[pl.BlockSpec(memory_space=pltpu.HBM)] * 6,
         out_specs=pl.BlockSpec(memory_space=pltpu.VMEM),
         scratch_shapes=[
@@ -462,7 +462,7 @@
         + [pltpu.SemaphoreType.DMA((CHUNKS,))]
         + [pltpu.SemaphoreType.DMA] * 6,
         compiler_params=pltpu.CompilerParams(
-            collective_id=0, has_side_effects=True, vmem_limit_bytes=215 * 256 * 1024
+            collective_id=0, has_side_effects=True, vmem_limit_bytes=54 * 1024 * 1024
         ),
     )(
         records.transpose(1, 2, 0, 3).reshape(traces, events, samples),

time: 61 us -> 60.2 us (0.987)
  local copies, waits for them, and re-layouts: 1.29 us -> 0.6 us
    unnamed x7 -> x1, local copies, waits for them, and re-layouts: 1.29 us -> 0.6 us
where the time goes in v6:
time: 60.2 us; the launch traced here: 60.1 us
  Pallas kernels  59.5 us (99%)
    pallas_call x1, Pallas kernels, shards(): pl.pallas_call(functools.partial(kernel, dims), out_shape=pltpu.VMEM((ele...  59.5 us

profile of v6, /device:TPU:1, one launch (start us, length us, event | category | flops | bytes accessed | tf_op | source)
XLA Modules:
  0.0 60.1 jit_solution(7651202919305195192)
XLA Ops:
  0.0 59.5 %shard_map.64 = f32[6,4,16]{2,1,0:T(4,128)S(1)} custom-call(bf16[54,4,1024]{2,1,0:T(4,128)(2,1)} %bitcast.9, bf16[108,3,1024]{2,1,0:T(4,128)(2,1)} %bitcast.8, bf16[1024,512]{1,0:T(8,128)(2,1)} %constant.2.clone.table_hbm, f32[1,256]{1,0:T(1,128)} %bitcast.10, s32[4,16]{1,0:T(4,128)} %cand_hbm.1, s32[1,64]{1,0:T(1,128)} %bitcast.11), custom_call_target="tpu_custom_call" | custom-call | tf_op jit(solution)/shard_map/pallas_call | solution.py:431
  59.5 0.6 %copy.8 = f32[4,16,6]{1,0,2:T(4,128)} copy(f32[4,16,6]{1,0,2:T(4,128)S(1)} %bitcast.7) | data formatting | bytes 3072
